TPU v7x, 32 devices: a whole 2x2x4 slice. The times are simulated.
32 devices in a mesh: expert: 4 (over y, x), context: 4 (over z), dp: 2 (over core).
Axes of the slice: x: 2, y: 2, z: 4, core: 2. Of those that a mesh axis runs over, the one named last changes fastest.
Arguments:
- layer_input: bfloat16 [8, 1024, 1536], P(('expert', 'dp'), 'context'), may hold values from -6 to 6
- gain_attn: bfloat16 [1536], P(('expert', 'context', 'dp')), may hold values from 0.5 to 1.5
- query_key_value_weight: bfloat16 [1536, 2048], P(('expert', 'context', 'dp')), may hold values from -0.15625 to 0.15625
- w_out: bfloat16 [1536, 1536], P(None, ('expert', 'context', 'dp')), may hold values from -2 to 2
- w_router: bfloat16 [1536, 8], P(('expert', 'context', 'dp')), may hold values from -0.078125 to 0.078125
- gain_ffn: bfloat16 [1536], P(('expert', 'context', 'dp')), may hold values from 0.5 to 1.5
- w_gate_up: bfloat16 [8, 1536, 1536], P('expert'), may hold values from -0.15625 to 0.15625
- w_down: bfloat16 [8, 768, 1536], P('expert'), may hold values from -0.625 to 0.625
- routes: int32 [8, 1024, 4], P(('expert', 'dp'), 'context'), may hold values from 0 to 7, all different within a row; in each aligned block of 256 rows (0 to 255, 256 to 511, ..., all dimensions but the last counted through in order) at most 256 rows name the same one
- d_out: bfloat16 [8, 1024, 1536], P(('expert', 'dp'), 'context'), may hold values from -6 to 6
Outputs:
- layer_output: bfloat16 [8, 1024, 1536], P(('expert', 'dp'), 'context')
- d_x: bfloat16 [8, 1024, 1536], P(('expert', 'dp'), 'context')
- g_gain_attn: float32 [1536], P(('expert', 'context', 'dp'))
- g_w_qkv: float32 [1536, 2048], P(('expert', 'context', 'dp'))
- g_w_out: float32 [1536, 1536], P(None, ('expert', 'context', 'dp'))
- g_w_router: float32 [1536, 8], P(('expert', 'context', 'dp'))
- g_gain_ffn: float32 [1536], P(('expert', 'context', 'dp'))
- g_w_gate_up: float32 [8, 1536, 1536], P('expert', ('context', 'dp'))
- g_w_down: float32 [8, 768, 1536], P('expert', None, ('context', 'dp'))
Inputs may be any that keep to these rules, and one draw needn't show every extreme that they name: `routes`: each token names 4 different experts. In each aligned block of 256 tokens (the tokens of one device) no expert is named by more than 256 tokens, a bound that some block reaches.
All inputs are finite; a program needn't handle non-finite values.
Results may differ from a plain program's by a relative error of at most 0.018.
Values may be sent and summed in bfloat16 or wider, within the bound.
A program may use at most 256 MiB of HBM per device.

v0:
```python
import functools
import math

import jax
import jax.numpy as jnp
from jax import lax
from jax.experimental import pallas as pl
from jax.experimental.pallas import tpu as pltpu
from jax.sharding import PartitionSpec as P

QUERY_HEADS = 12
KEY_VALUE_HEADS = 2
HEAD_DIMENSION = 128
TOP = 4
EXP_DEV = 2

EPSILON = 1e-06
ROPE_BASE = 10000.0
MASKED = -1e30

F32 = jnp.float32
BF16 = jnp.bfloat16


def rope_tables(positions, width):
    halfway = width // 2
    fraction = jnp.arange(halfway, dtype=jnp.float32) * (2.0 / width)
    frequency = jnp.exp(-math.log(ROPE_BASE) * fraction)
    angles = positions.astype(jnp.float32)[:, None] * frequency[None, :]
    cosine_values = jnp.cos(angles)
    sine_values = jnp.sin(angles)
    return (
        jnp.concatenate([cosine_values, cosine_values], -1),
        jnp.concatenate([sine_values, sine_values], -1),
    )


def rotate_half(values, cosine_values, sine_values):
    halfway = values.shape[-1] // 2
    turned = jnp.concatenate([-values[..., halfway:], values[..., :halfway]], -1)
    return values * cosine_values[:, None, :] + turned * sine_values[:, None, :]


def rotate_back(grads, cosine_values, sine_values):
    halfway = grads.shape[-1] // 2
    scaled = grads * sine_values[:, None, :]
    turned = jnp.concatenate([scaled[..., halfway:], -scaled[..., :halfway]], -1)
    return grads * cosine_values[:, None, :] + turned


def dot_nt(a, b):
    return lax.dot_general(a, b, (((1,), (1,)), ((), ())), preferred_element_type=F32)


def dot_tn(a, b):
    return lax.dot_general(a, b, (((0,), (0,)), ((), ())), preferred_element_type=F32)


def dot_nn(a, b):
    return jnp.dot(a, b, preferred_element_type=F32)


def masked_probs(first_row, query, key):
    scores = dot_nt(query, key) * (HEAD_DIMENSION**-0.5)
    rows = first_row + lax.broadcasted_iota(jnp.int32, scores.shape, 0)
    columns = lax.broadcasted_iota(jnp.int32, scores.shape, 1)
    scores = jnp.where(columns <= rows, scores, MASKED)
    expd = jnp.exp(scores - jnp.max(scores, axis=-1, keepdims=True))
    return expd / jnp.sum(expd, axis=-1, keepdims=True)


def attend_forward_kernel(first_ref, query_ref, key_ref, value_ref, heads_ref):
    probs = masked_probs(first_ref[0], query_ref[...], key_ref[...])
    heads_ref[...] = dot_nn(probs.astype(BF16), value_ref[...]).astype(BF16)


def attend_forward(first_row, query, key_value):
    tokens, width = query.shape
    length = key_value.shape[0]
    group = QUERY_HEADS // KEY_VALUE_HEADS
    size = HEAD_DIMENSION
    return pl.pallas_call(
        attend_forward_kernel,
        grid_spec=pltpu.PrefetchScalarGridSpec(
            num_scalar_prefetch=1,
            grid=(QUERY_HEADS,),
            in_specs=[
                pl.BlockSpec((tokens, size), lambda h, s: (0, h)),
                pl.BlockSpec((length, size), lambda h, s: (0, h // group)),
                pl.BlockSpec((length, size), lambda h, s: (0, KEY_VALUE_HEADS + h // group)),
            ],
            out_specs=pl.BlockSpec((tokens, size), lambda h, s: (0, h)),
        ),
        out_shape=jax.ShapeDtypeStruct((tokens, width), BF16),
        compiler_params=pltpu.CompilerParams(vmem_limit_bytes=32 * 1024 * 1024),
        cost_estimate=pl.CostEstimate(
            flops=4 * tokens * length * width, bytes_accessed=4 * tokens * width, transcendentals=0
        ),
    )(first_row, query, key_value, key_value)


def attend_backward_kernel(
    first_ref, query_ref, key_ref, value_ref, grad_ref, d_query_ref, d_key_ref, d_value_ref
):
    query, key, value, grad = query_ref[...], key_ref[...], value_ref[...], grad_ref[...]
    probs = masked_probs(first_ref[0], query, key)
    d_probs = dot_nt(grad, value)
    inner = jnp.sum(probs * d_probs, axis=-1, keepdims=True)
    d_raw = (probs * (d_probs - inner) * (HEAD_DIMENSION**-0.5)).astype(BF16)
    d_query_ref[...] = dot_nn(d_raw, key)
    d_key = dot_tn(d_raw, query)
    d_value = dot_tn(probs.astype(BF16), grad)

    @pl.when(pl.program_id(1) == 0)
    def _():
        d_key_ref[...] = d_key
        d_value_ref[...] = d_value

    @pl.when(pl.program_id(1) > 0)
    def _():
        d_key_ref[...] += d_key
        d_value_ref[...] += d_value


def attend_backward(first_row, query, key_value, grad):
    tokens, width = query.shape
    length = key_value.shape[0]
    group = QUERY_HEADS // KEY_VALUE_HEADS
    size = HEAD_DIMENSION
    row_spec = pl.BlockSpec((tokens, size), lambda j, g, s: (0, j * group + g))
    return pl.pallas_call(
        attend_backward_kernel,
        grid_spec=pltpu.PrefetchScalarGridSpec(
            num_scalar_prefetch=1,
            grid=(KEY_VALUE_HEADS, group),
            in_specs=[
                row_spec,
                pl.BlockSpec((length, size), lambda j, g, s: (0, j)),
                pl.BlockSpec((length, size), lambda j, g, s: (0, KEY_VALUE_HEADS + j)),
                row_spec,
            ],
            out_specs=[
                row_spec,
                pl.BlockSpec((length, size), lambda j, g, s: (0, j)),
                pl.BlockSpec((length, size), lambda j, g, s: (0, j)),
            ],
        ),
        out_shape=[
            jax.ShapeDtypeStruct((tokens, width), F32),
            jax.ShapeDtypeStruct((length, KEY_VALUE_HEADS * size), F32),
            jax.ShapeDtypeStruct((length, KEY_VALUE_HEADS * size), F32),
        ],
        compiler_params=pltpu.CompilerParams(vmem_limit_bytes=32 * 1024 * 1024),
        cost_estimate=pl.CostEstimate(
            flops=10 * tokens * length * width, bytes_accessed=8 * tokens * width, transcendentals=0
        ),
    )(first_row, query, key_value, key_value, grad)


def exchange(values, axis, mask):
    size = lax.axis_size(axis)
    return lax.ppermute(values, axis, [(i, i ^ mask) for i in range(size)])


def axis_masks(axis):
    size = lax.axis_size(axis)
    masks, bit = [], 1
    while bit < size:
        masks.append(bit)
        bit *= 2
    return masks


def cube_gather(values, axis, masks):
    held = {0: values}
    for mask in masks:
        for r, block in list(held.items()):
            held[r ^ mask] = exchange(block, axis, mask)
    return [held[r] for r in range(lax.axis_size(axis))]


def cube_scatter(blocks, axis, masks):
    held = dict(enumerate(blocks))
    for mask in masks:
        kept = {}
        for r in list(held):
            if not r & mask:
                arrived = exchange(held[r ^ mask].astype(BF16), axis, mask)
                kept[r] = held[r].astype(F32) + arrived.astype(F32)
        held = kept
    return held[0]


def line_steps(values, axis, up):
    size = lax.axis_size(axis)
    pairs = [(i, i + 1) if up else (i + 1, i) for i in range(size - 1)]
    return lax.ppermute(values, axis, pairs)


def line_gather(values, axis, both=True):
    size = lax.axis_size(axis)
    me = lax.axis_index(axis)
    result = jnp.zeros((size + 1,) + values.shape, values.dtype)
    result = lax.dynamic_update_index_in_dim(result, values, me, 0)
    up = down = values
    for step in range(1, size):
        up = line_steps(up, axis, True)
        result = lax.dynamic_update_index_in_dim(
            result, up, jnp.where(me - step >= 0, me - step, size), 0
        )
        if both:
            down = line_steps(down, axis, False)
            result = lax.dynamic_update_index_in_dim(result, down, jnp.minimum(me + step, size), 0)
    return result[:size]


def line_scatter(take, axis, up=True, down=True):
    size = lax.axis_size(axis)
    me = lax.axis_index(axis)
    total = take(me).astype(F32)
    for active, sign in ((up, 1), (down, -1)):
        if not active:
            continue
        arrived = None
        for step in range(1, size):
            block = take((me + sign * (size - step)) % size).astype(F32)
            if arrived is not None:
                block = block + arrived.astype(F32)
            arrived = line_steps(block.astype(BF16), axis, sign > 0)
        total = total + arrived.astype(F32)
    return total


def gather_rows(shard):
    ne, nc, nd = (lax.axis_size(a) for a in ("expert", "context", "dp"))
    rows, width = shard.shape
    lines = line_gather(shard, "context")
    masks = axis_masks("expert")
    half = width // 256 * 128
    parts = [lines[..., :half], lines[..., half:]]
    me = lax.axis_index("expert")
    result = jnp.zeros((ne, nc, rows, width), shard.dtype)
    for start, part, order in ((0, parts[0], masks), (half, parts[1], masks[::-1])):
        for r, block in enumerate(cube_gather(part, "expert", order)):
            result = lax.dynamic_update_slice(result, block[None], (me ^ r, 0, 0, start))
    core = lax.axis_index("dp")
    whole = jnp.zeros((ne, nc, nd, rows, width), shard.dtype)
    for r, block in enumerate(cube_gather(result, "dp", axis_masks("dp"))):
        whole = lax.dynamic_update_slice(whole, block[:, :, None], (0, 0, core ^ r, 0, 0))
    return whole.reshape(-1, width)


def scatter_rows(grad):
    ne, nc, nd = (lax.axis_size(a) for a in ("expert", "context", "dp"))
    width = grad.shape[-1]
    rows = grad.shape[0] // (ne * nc * nd)
    blocks = grad.reshape(ne, nc, nd, rows, width)
    core, me = lax.axis_index("dp"), lax.axis_index("expert")
    mine = cube_scatter(
        [
            lax.dynamic_index_in_dim(blocks, core ^ r, 2, keepdims=False)
            for r in range(nd)
        ],
        "dp",
        axis_masks("dp"),
    )
    masks = axis_masks("expert")
    half = width // 256 * 128
    sums = []
    for part, order in ((mine[..., :half], masks), (mine[..., half:], masks[::-1])):
        sums.append(
            cube_scatter(
                [lax.dynamic_index_in_dim(part, me ^ r, 0, keepdims=False) for r in range(ne)],
                "expert",
                order,
            )
        )
    lines = jnp.concatenate(sums, -1)
    return line_scatter(
        lambda j: lax.dynamic_index_in_dim(lines, j, 0, keepdims=False), "context"
    )


def plane_gather(rows):
    masks = axis_masks("expert")
    half = rows.shape[-1] // 2
    left = cube_gather(rows[:, :half], "expert", masks)
    right = cube_gather(rows[:, half:], "expert", masks[::-1])
    return jnp.concatenate([jnp.concatenate(p, -1) for p in zip(left, right)], 0)


def plane_scatter(partial, tokens):
    masks = axis_masks("expert")
    size = lax.axis_size("expert")
    half = partial.shape[-1] // 2
    blocks = partial.reshape(size, tokens, -1)
    left = cube_scatter([blocks[r, :, :half] for r in range(size)], "expert", masks)
    right = cube_scatter([blocks[r, :, half:] for r in range(size)], "expert", masks[::-1])
    return jnp.concatenate([left, right], -1)


MESH = pl.DeviceIdType.MESH
MIB = 1024 * 1024
SMALL = 128
GATE_ROWS = 16


def flip(index, mask):
    bit = 1
    while bit <= mask:
        if mask & bit:
            index = index + bit - 2 * bit * lax.rem(lax.div(index, bit), 2)
        bit *= 2
    return index


class Wire:
    def __init__(self, sends, recvs):
        self.sends, self.recvs = sends, recvs
        self.n_sends = self.n_recvs = 0
        self.open = []

    def slots(self, count):
        first = self.n_recvs
        self.n_recvs += count
        return first

    def start(self, src, dst, recv, device, when=None):
        number = self.n_sends
        self.n_sends += 1

        def copy():
            return pltpu.make_async_remote_copy(
                src_ref=src() if callable(src) else src,
                dst_ref=dst() if callable(dst) else dst,
                send_sem=self.sends.at[number],
                recv_sem=self.recvs.at[recv],
                device_id=device,
                device_id_type=MESH,
            )

        guard(when, lambda: copy().start())
        self.open.append((when, copy))

    def arrived(self, dst, recv, device):
        pltpu.make_async_remote_copy(
            src_ref=dst,
            dst_ref=dst,
            send_sem=self.sends.at[0],
            recv_sem=self.recvs.at[recv],
            device_id=device,
            device_id_type=MESH,
        ).wait_recv()

    def finish(self):
        for when, copy in self.open:
            guard(when, lambda copy=copy: copy().wait_send())
        self.open = []


def guard(when, action):
    if when is None:
        action()
    else:
        pl.when(when)(action)


def add_into(dest, source, steps=4):
    rows = dest.shape[0] // steps

    @pl.loop(0, steps)
    def _(n):
        here = pl.ds(pl.multiple_of(n * rows, rows), rows)
        dest[here] = (dest[here].astype(F32) + source[here].astype(F32)).astype(BF16)


def greet(targets):
    barrier = pltpu.get_barrier_semaphore()
    for device, when in targets:
        guard(
            when,
            lambda device=device: pl.semaphore_signal(
                barrier, inc=1, device_id=device, device_id_type=MESH
            ),
        )
    count = sum(1 if when is None else when.astype(jnp.int32) for _, when in targets)
    pl.semaphore_wait(barrier, count)


def plane_ids(e):
    return {m: {"expert": flip(e, m)} for m in (1, 2, 3)}


class RowsGather:
    def __init__(self, wire, ref, e, z, c, nc, half):
        self.wire, self.ref, self.e, self.z, self.c, self.nc = wire, ref, e, z, c, nc
        self.cols = (pl.ds(0, half), pl.ds(half, ref.shape[-1] - half))
        self.line = wire.slots(nc)
        self.plane = wire.slots(nc * 6)
        self.core = wire.slots(nc)
        self.ids = plane_ids(e)

    def go(self, *steps):
        for step in steps:
            action = {"l": self.pass_on, "s": self.spread, "f": self.forward, "h": self.share, "c": self.complete}
            action[step[0]](*map(int, step[1:]))

    def shard(self, k):
        if k < 2:
            return flip(self.z, k)
        inner = (self.z > 0) & (self.z < self.nc - 1)
        return jnp.where(inner, flip(self.z, 5 - k), flip(self.z, k))

    def at(self, r, zs, half):
        return self.ref.at[flip(self.e, r), zs, self.c, :, self.cols[half]]

    def slot(self, k, r, half):
        return self.plane + k * 6 + (r - 1) * 2 + half

    def pass_on(self, k):
        wire, z, nc = self.wire, self.z, self.nc
        zs = self.shard(k)
        whole = self.ref.at[self.e, zs, self.c]
        if k:
            wire.arrived(whole, self.line + zs, {"context": zs})
        wire.start(
            whole, whole, self.line + zs, {"context": z + 1}, when=(zs <= z) & (z < nc - 1)
        )
        wire.start(whole, whole, self.line + zs, {"context": z - 1}, when=(zs >= z) & (z > 0))

    def spread(self, k):
        zs = self.shard(k)
        for half, mask in ((0, 1), (1, 2), (1, 1), (0, 2)):
            part = self.at(0, zs, half)
            self.wire.start(part, part, self.slot(k, mask, half), self.ids[mask])

    def forward(self, k):
        zs = self.shard(k)
        for half, mask in ((0, 1), (1, 2)):
            part = self.at(mask, zs, half)
            self.wire.arrived(part, self.slot(k, mask, half), self.ids[mask])
            self.wire.start(part, part, self.slot(k, 3, half), self.ids[3 - mask])

    def share(self, k):
        zs = self.shard(k)
        for r, half in ((1, 1), (2, 0), (3, 0), (3, 1)):
            self.wire.arrived(self.at(r, zs, half), self.slot(k, r, half), self.ids[r])
        part = self.ref.at[:, zs, self.c]
        self.wire.start(part, part, self.core + k, {"dp": 1 - self.c})

    def complete(self):
        for k in range(self.nc):
            zs = self.shard(k)
            self.wire.arrived(self.ref.at[:, zs, 1 - self.c], self.core + k, {"dp": 1 - self.c})


class PlaneGather:
    def __init__(self, wire, ref, e, own=None):
        self.wire, self.ref, self.own = wire, ref, own
        self.half = ref.shape[-1] // 2
        self.ids = plane_ids(e)
        self.first = wire.slots(6)

    def at(self, r, half):
        columns = pl.ds(half * self.half, self.half)
        if r == 0 and self.own is not None:
            return self.own.at[:, columns]
        return self.ref.at[r, :, columns]

    def slot(self, r, half):
        return self.first + (r - 1) * 2 + half

    def send(self, r, half, to, mask):
        self.wire.start(
            lambda: self.at(r, half), lambda: self.at(to, half), self.slot(to, half), self.ids[mask]
        )

    def spread(self):
        for half, mask in ((0, 1), (1, 2), (1, 1), (0, 2)):
            self.send(0, half, mask, mask)

    def forward(self):
        for half, mask in ((0, 1), (1, 2)):
            self.wire.arrived(self.at(mask, half), self.slot(mask, half), self.ids[mask])
            self.send(mask, half, 3, 3 - mask)

    def near(self, r):
        half = 1 if r == 1 else 0
        self.wire.arrived(self.at(r, half), self.slot(r, half), self.ids[r])

    def far(self):
        for half in (0, 1):
            self.wire.arrived(self.at(3, half), self.slot(3, half), self.ids[3])

    def complete(self):
        self.near(1)
        self.near(2)
        self.far()


def causal(scores, first_row):
    place = lax.broadcasted_iota(jnp.int32, scores.shape, 0)
    row = first_row + lax.broadcasted_iota(jnp.int32, scores.shape, 1)
    return jnp.where(place <= row, scores, MASKED)


def swap_halves(values):
    return pltpu.roll(values, HEAD_DIMENSION // 2, 1)


class PlaneScatter:
    def __init__(self, wire, land, ids):
        self.wire, self.land, self.ids, self.part = wire, land, ids, None
        self.half = land.shape[-1]
        self.first = wire.slots(6)

    def send(self, source, mask, slot):
        self.wire.start(source, lambda: self.land.at[slot], self.first + slot, self.ids[mask])

    def near(self, r):
        self.send(self.part(r, r - 1), r, r - 1)

    def far(self):
        self.send(self.part(3, 0), 1, 2)
        self.send(self.part(3, 1), 2, 3)

    def relay(self, part=None):
        for half, r in ((0, 2), (1, 1)):
            slot = 2 + half
            self.wire.arrived(self.land.at[slot], self.first + slot, self.ids[3 - r])
            take = part or self.part
            mine = take(r, half)
            add_into(mine, self.land.at[slot])
            self.send(lambda r=r, half=half, take=take: take(r, half), r, 4 + half)

    def total(self, own):
        for slot, half, mask in ((0, 0, 1), (1, 1, 2), (4, 0, 2), (5, 1, 1)):
            self.wire.arrived(self.land.at[slot], self.first + slot, self.ids[mask])
            columns = pl.ds(half * self.half, self.half)
            rows = own.shape[0] // 4

            @pl.loop(0, 4)
            def _(n):
                here = pl.ds(pl.multiple_of(n * rows, rows), rows)
                own[here, columns] += self.land[slot, here].astype(F32)


class LineSum:
    def __init__(self, wire, block, land, z, nc, up=True):
        self.wire, self.block, self.land, self.z, self.nc, self.up = wire, block, land, z, nc, up
        self.first = wire.slots(nc)

    def clear(self):
        for slot in range(self.nc):

            def zero(slot=slot):
                self.land[slot] = jnp.zeros(self.land.shape[1:], BF16)

            pl.when(slot == self.z if self.up else slot <= self.z)(zero)

    def send(self):
        z = self.z
        for d in range(self.nc - 1, 0, -1):
            self.leave(z - d, z >= d)
            if self.up:
                self.leave(z + d, z + d < self.nc)

    def leave(self, j, wanted):
        self.wire.start(
            self.block(j), self.land.at[self.z], self.first + self.z, {"context": j}, when=wanted
        )

    def total(self):
        z = self.z
        for d in range(1, self.nc):
            for source, wanted in ((z + d, z + d < self.nc), (z - d, z >= d))[: 1 + self.up]:

                def wait(source=source):
                    self.wire.arrived(
                        self.land.at[source], self.first + source, {"context": source}
                    )

                pl.when(wanted)(wait)
        total = self.block(z)[...].astype(F32)
        for slot in range(self.nc):
            total = total + self.land[slot].astype(F32)
        return total


class RowsScatter:
    def __init__(self, wire, buf, core, plane, lines, e, z, c, nc, start, width, half):
        self.wire, self.buf, self.core, self.plane = wire, buf, core, plane
        self.e, self.c = e, c
        self.all = pl.ds(start, width)
        self.cols = (pl.ds(start, half), pl.ds(start + half, width - half))
        self.ids = plane_ids(e)
        self.core_slot = wire.slots(1)
        self.first = wire.slots(6)
        rows = buf.shape[2] // nc
        self.line = LineSum(
            wire,
            lambda j: buf.at[c, e, pl.ds(pl.multiple_of(j * rows, rows), rows), self.all],
            lines,
            z,
            nc,
        )

    def share(self):
        self.wire.start(
            self.buf.at[1 - self.c, :, :, self.all], self.core, self.core_slot, {"dp": 1 - self.c}
        )

    def at(self, r, half):
        return self.buf.at[self.c, flip(self.e, r), :, self.cols[half]]

    def send(self, r, half, mask, slot):
        self.wire.start(
            self.at(r, half), self.plane(slot, half), self.first + slot, self.ids[mask]
        )

    def merge(self, before=None):
        self.wire.arrived(self.core, self.core_slot, {"dp": 1 - self.c})
        for r in (3, 1, 2, 0):
            block = flip(self.e, r)
            part = self.buf.at[self.c, block, :, self.all]
            add_into(part, self.core.at[block])
            if r == 3:
                if before is not None:
                    before()
                self.send(3, 0, 1, 2)
                self.send(3, 1, 2, 3)
            elif r:
                self.send(r, r - 1, r, r - 1)

    def add(self, r, half, slot, mask):
        land = self.plane(slot, half)
        self.wire.arrived(land, self.first + slot, self.ids[mask])
        add_into(self.at(r, half), land)

    def relay(self):
        for half, r in ((0, 2), (1, 1)):
            self.add(r, half, 2 + half, 3 - r)
            self.send(r, half, r, 4 + half)

    def total(self):
        for slot, half, mask in ((0, 0, 1), (1, 1, 2), (4, 0, 2), (5, 1, 1)):
            self.add(0, half, slot, mask)


class ExpertLine:
    def __init__(self, wire, base, land, sems, z, nc):
        self.wire, self.base, self.land = wire, base, land
        self.ins, self.out, self.sems, self.z, self.nc = None, None, sems, z, nc
        self.end = (z == 0) | (z == nc - 1)
        self.inner = jnp.logical_not(self.end)
        self.width = base.shape[-1] // EXP_DEV
        self.first = wire.slots((nc + 1) * EXP_DEV)
        self.sent = []

    def part(self, ref, j, i):
        return ref.at[j, :, pl.ds(i * self.width, self.width)]

    def combine(self, sources, stores):
        out, step = self.out, self.ins.shape[2]
        count = sources[0].shape[0] // step

        def loads(p):
            rows = pl.ds(p * step, step)
            return [
                pltpu.make_async_copy(source.at[rows], self.ins.at[k, p], self.sems.at[4 * k + p])
                for k, source in enumerate(sources)
            ]

        def store(p):
            pairs = stores(pl.ds(p * step, step), out.at[p % 2])
            return [
                pltpu.make_async_copy(source, dest, self.sems.at[16 + 2 * n + p % 2])
                for n, (source, dest) in enumerate(pairs)
            ]

        for p in range(count):
            for copy in loads(p):
                copy.start()
        for p in range(count):
            for copy in loads(p):
                copy.wait()
            if p > 1:
                for copy in store(p - 2):
                    copy.wait()
            total = self.ins[0, p].astype(F32)
            for k in range(1, len(sources)):
                total = total + self.ins[k, p].astype(F32)
            out[p % 2] = total.astype(out.dtype)
            for copy in store(p):
                copy.start()
        for p in range(max(0, count - 2), count):
            for copy in store(p):
                copy.wait()

    def copy(self, i, r, number):
        target, slot = flip(self.z, r), self.z
        if r == 3:
            target = jnp.where(self.end, flip(self.z, 1), target)
            slot = jnp.where(self.end, self.nc, slot)
        return pltpu.make_async_remote_copy(
            src_ref=self.part(self.base, flip(self.z, r), i),
            dst_ref=self.part(self.land, slot, i),
            send_sem=self.wire.sends.at[number],
            recv_sem=self.wire.recvs.at[self.first + slot * EXP_DEV + i],
            device_id={"context": target},
            device_id_type=MESH,
        )

    def send(self, i, r, when=None):
        number = len(self.sent)
        guard(when, self.copy(i, r, number).start)
        self.sent.append((when, i, r, number))

    def finish(self):
        for when, i, r, number in self.sent:
            guard(when, self.copy(i, r, number).wait_send)

    def arrived(self, slot, i):
        land = self.part(self.land, slot, i)
        self.wire.arrived(land, self.first + slot * EXP_DEV + i, {"context": self.z})

    def relay_loads(self, i, p):
        step = self.ins.shape[2]
        rows = pl.ds(p * step, step)
        sources = (self.part(self.base, flip(self.z, 2), i), self.part(self.land, self.nc, i))
        return [
            pltpu.make_async_copy(
                source.at[rows], self.ins.at[k, p], self.sems.at[4 * k + p]
            )
            for k, source in enumerate(sources)
        ]

    def relay_store(self, i, p):
        step = self.ins.shape[2]
        mine = self.part(self.base, flip(self.z, 2), i).at[pl.ds(p * step, step)]
        return pltpu.make_async_copy(self.ins.at[0, p], mine, self.sems.at[16 + p])

    def relay_steps(self):
        return range(self.base.shape[1] // self.ins.shape[2])

    def relay_begin(self, i):
        self.relayed = i

        def begin():
            self.arrived(self.nc, i)
            for p in self.relay_steps():
                for copy in self.relay_loads(i, p):
                    copy.start()

        pl.when(self.inner)(begin)

    def relay_add(self):
        i = self.relayed

        def add():
            for p in self.relay_steps():
                for copy in self.relay_loads(i, p):
                    copy.wait()
                a, b = (self.ins[k, p].astype(F32) for k in range(2))
                self.ins[0, p] = (a + b).astype(BF16)
                self.relay_store(i, p).start()

        pl.when(self.inner)(add)

    def relay_send(self, i):
        def wait():
            for p in self.relay_steps():
                self.relay_store(i, p).wait()

        pl.when(self.inner)(wait)
        self.send(i, 2, when=self.inner)

    def last(self, i, results):
        z = self.z
        sources = [self.part(self.base, z, i)]
        for r in (1, 2):
            self.arrived(flip(z, r), i)
            sources.append(self.part(self.land, flip(z, r), i))

        def stores(rows, wide):
            pairs, first = [], 0
            for result in results:
                columns = pl.ds(first, result.shape[-1])
                pairs.append((wide.at[:, columns], result.at[i, rows]))
                first += result.shape[-1]
            return pairs

        pl.when(self.end)(lambda: self.combine(sources, stores))

        def inner():
            self.arrived(flip(z, 3), i)
            self.combine(sources + [self.part(self.land, flip(z, 3), i)], stores)

        pl.when(self.inner)(inner)


def layer_kernel(
    nc,
    experts,
    cos_ref,
    sin_ref,
    routes_ref,
    qkv_ref,
    small_ref,
    wo_shard_ref,
    x_hbm,
    d_out_hbm,
    w_gu_hbm,
    w_dn_hbm,
    layer_hbm,
    d_x_hbm,
    sum_q_ref,
    sum_o_ref,
    sum_gu_hbm,
    sum_dn_hbm,
    base_hbm,
    land_hbm,
    y_hbm,
    wq_hbm,
    wo_hbm,
    cot_hbm,
    inputs_hbm,
    query_hbm,
    heads_hbm,
    hidden_hbm,
    wk_all,
    kv_ref,
    gate_all,
    gates_ref,
    gains_ref,
    x_all,
    y_land,
    dx_land,
    core_land,
    plane_q,
    plane_k,
    lines_o,
    lines_q,
    lines_k,
    dkv_land,
    d_in_ref,
    dg_lanes,
    dg_part,
    dg_land,
    sends_f,
    recvs_f,
    sends_c,
    recvs_c,
    sends_x,
    recvs_x,
    sends_1,
    recvs_1,
    sends_2,
    recvs_2,
    sends_e,
    recvs_e,
    hand_sends,
    hand_recvs,
    stage_sems,
    load_sems,
    out_sems,
    sum_sems,
    y_sems,
    credits,
):
    e, z, c = (lax.axis_index(a) for a in ("expert", "context", "dp"))
    size = HEAD_DIMENSION
    blocks, tokens, width = cot_hbm.shape
    ff = w_dn_hbm.shape[1]
    query_width = QUERY_HEADS * size
    key_width = KEY_VALUE_HEADS * size
    qkv_width = query_width + 2 * key_width
    rest = wk_all.shape[-1]
    grad_width = base_hbm.shape[-1]
    ids = plane_ids(e)
    sibling = {"dp": 1 - c}
    bottom, even, odd, top = z == 0, lax.rem(z, 2) == 0, lax.rem(z, 2) == 1, z == nc - 1
    wire_1, wire_2, wire_e = Wire(sends_1, recvs_1), Wire(sends_2, recvs_2), Wire(sends_e, recvs_e)
    expert = ExpertLine(wire_e, base_hbm, land_hbm, sum_sems, z, nc)
    wire_c = Wire(sends_c, recvs_c)
    gather_cot = PlaneGather(wire_c, cot_hbm, e, d_out_hbm)
    wire_x = Wire(sends_x, recvs_x)
    gather = PlaneGather(wire_x, x_all, e)
    scatter_dx = PlaneScatter(wire_1, dx_land, ids)
    scatter_y = PlaneScatter(wire_2, y_land, ids)
    dg_slot = wire_1.slots(3)

    def front_phase(wq_ref, wo_ref, x_ref, inputs_ref, query_ref, heads_ref, hidden_ref, kv_scr, q_scr):
        wire = Wire(sends_f, recvs_f)
        kv_width = 2 * key_width
        load_x = pltpu.make_async_copy(x_hbm, x_ref, load_sems.at[0])
        load_x.start()
        wq_ref[e, z, c] = qkv_ref[:, pl.ds(0, query_width)]
        wo_ref[e, z, c] = wo_shard_ref[...]
        wk_all[e, z, c, :, pl.ds(0, kv_width)] = qkv_ref[:, pl.ds(query_width, kv_width)]
        wk_all[e, z, c, :, pl.ds(kv_width, SMALL)] = small_ref[...]
        greet(
            [(ids[m], None) for m in (1, 2, 3)]
            + [(sibling, None)]
            + [({"context": z + d}, z + d < nc) for d in range(1, nc)]
            + [({"context": z - d}, z >= d) for d in range(1, nc)]
        )
        gather_k = RowsGather(wire, wk_all, e, z, c, nc, 256)
        gather_q = RowsGather(wire, wq_ref, e, z, c, nc, 768)
        gather_o = RowsGather(wire, wo_ref, e, z, c, nc, 768)
        gather_k.go("l0", "s0")
        gather_q.go("s0")
        gather_k.go("l1", "s1", "f0", "l2", "s2")
        gather_q.go("l0")
        gather_k.go("f1", "h0", "l3", "s3")
        gather_q.go("l1", "s1")
        gather_o.go("l0")
        gather_k.go("f2", "h1", "f3")
        gather_q.go("l2", "s2")
        gather_k.go("h2")
        gather_o.go("l1")
        gather_q.go("f0")
        gather_k.go("h3")
        gather_q.go("l3", "s3")
        gather_k.go("c")
        load_x.wait()
        rows = x_ref[...].astype(F32)
        scale1 = lax.rsqrt(jnp.mean(rows * rows, -1, keepdims=True) + EPSILON)

        small = wk_all[:, :, :, :, pl.ds(kv_width, SMALL)].reshape(width, SMALL)
        small = jnp.transpose(small.astype(F32))
        gain_first, gain_second = small[experts : experts + 1], small[experts + 1 : experts + 2]
        gains_ref[0:1] = gain_first
        gains_ref[1:2] = gain_second
        inputs_ref[...] = (rows * scale1 * gain_first).astype(BF16)
        kv_scr[...] = dot_nn(inputs_ref[...], wk_all[...].reshape(width, kv_width + SMALL))

        def turned(head):
            return (head * cos_ref[...] + swap_halves(head) * sin_ref[...]).astype(BF16)

        line = wire.slots(KEY_VALUE_HEADS * nc)
        for j in range(KEY_VALUE_HEADS):
            kv_ref[j, z, :, pl.ds(0, size)] = turned(kv_scr[:, pl.ds(j * size, size)])
            value = kv_scr[:, pl.ds(kv_width // 2 + j * size, size)]
            kv_ref[j, z, :, pl.ds(size, size)] = value.astype(BF16)
            mine = kv_ref.at[j, z]
            for d in range(nc - 1, 0, -1):
                wire.start(mine, mine, line + j * nc + z, {"context": z + d}, when=z + d < nc)

        def keys_here(j):
            for d in range(1, nc):

                def wait(d=d):
                    wire.arrived(kv_ref.at[j, z - d], line + j * nc + z - d, {"context": z - d})

                pl.when(z >= d)(wait)

        outs = [
            pltpu.make_async_copy(source, dest, out_sems.at[n])
            for n, (source, dest) in enumerate(
                (
                    (inputs_ref, inputs_hbm),
                    (query_ref, query_hbm),
                    (heads_ref, heads_hbm),
                    (hidden_ref, hidden_hbm),
                    (wq_ref, wq_hbm),
                    (wo_ref, wo_hbm),
                )
            )
        ]
        outs[0].start()
        for later in range(1, nc):

            def clear(later=later):
                for j in range(KEY_VALUE_HEADS):
                    kv_ref[j, z + later] = jnp.zeros(kv_ref.shape[2:], BF16)

            pl.when(z + later < nc)(clear)
        gather_q.go("f1", "f2", "h0")
        gather_o.go("s0")
        gather_q.go("f3", "h1")
        gather_o.go("s1")
        gather_q.go("h2", "h3", "c")
        outs[4].start()
        gather_o.go("f0", "f1")
        gather_cot.spread()

        @pl.loop(0, query_width // 256)
        def _(n):
            columns = pl.ds(pl.multiple_of(n * 256, 256), 256)
            q_scr[:, columns] = dot_nn(
                inputs_ref[...], wq_ref[:, :, :, :, columns].reshape(width, 256)
            )

        @pl.loop(0, QUERY_HEADS)
        def _(h):
            columns = pl.ds(pl.multiple_of(h * size, size), size)
            query_ref[:, columns] = turned(q_scr[:, columns])

        outs[1].start()

        logits = kv_scr[:, pl.ds(kv_width, SMALL)]
        lanes = lax.broadcasted_iota(jnp.int32, logits.shape, 1)
        routes = jnp.concatenate(
            [routes_ref[...].astype(F32), jnp.zeros((SMALL - TOP, tokens), F32)], 0
        )
        routes = jnp.transpose(routes).astype(jnp.int32)
        named = lanes == routes[:, 0:1]
        for k in range(1, TOP):
            named = named | (lanes == routes[:, k : k + 1])
        logits = jnp.where(named, logits, MASKED)
        expd = jnp.exp(logits - jnp.max(logits, -1, keepdims=True))
        gates = expd / jnp.sum(expd, -1, keepdims=True)
        gate_all[0] = jnp.transpose(gates)[:GATE_ROWS]
        gate_slot = wire.slots(3)
        for r in (1, 2, 3):
            wire.start(gate_all.at[0], gate_all.at[r], gate_slot + r - 1, ids[r])

        length = nc * tokens
        group = QUERY_HEADS // KEY_VALUE_HEADS

        def attend(first, last):
            j = first // group
            key = kv_ref[j, :, :, pl.ds(0, size)].reshape(length, size)
            value = kv_ref[j, :, :, pl.ds(size, size)].reshape(length, size)
            value_turned = jnp.transpose(value)

            @pl.loop(first, last)
            def _(h):
                column = pl.multiple_of(h * size, size)
                scores = causal(dot_nt(key, query_ref[:, pl.ds(column, size)]), z * tokens)
                largest = jnp.max(scores, 0, keepdims=True)
                expd = jnp.exp((scores - largest) * (size**-0.5))
                total = jnp.sum(expd, 0, keepdims=True)
                mixed = dot_nn(value_turned, expd.astype(BF16)) / total
                heads_ref[:, pl.ds(column, size)] = jnp.transpose(mixed).astype(BF16)

        half = group // 2
        keys_here(0)
        attend(0, half)
        gather_o.go("l2", "s2")
        attend(half, group)
        gather_o.go("l3", "s3", "f2", "h0")
        keys_here(1)
        attend(group, group + half)
        gather_o.go("f3", "h1")
        attend(group + half, QUERY_HEADS)
        gather_o.go("h2")
        gather_cot.forward()
        gather_o.go("h3", "c")
        outs[5].start()
        outs[2].start()
        part = width // wo_ref.shape[0]
        for block in range(wo_ref.shape[0]):
            weight = wo_ref[block].reshape(part, width)
            columns = pl.ds(block * part, part)
            hidden_ref[:, columns] = x_ref[:, columns].astype(F32) + dot_nt(heads_ref[...], weight)
        hidden = hidden_ref[...]
        scale2 = lax.rsqrt(jnp.mean(hidden * hidden, -1, keepdims=True) + EPSILON)
        x_all[0] = (hidden * scale2 * gains_ref[1:2]).astype(BF16)
        gather.spread()
        outs[3].start()
        for r in (1, 2, 3):
            wire.arrived(gate_all.at[r], gate_slot + r - 1, ids[r])
        for r in range(gate_all.shape[0]):
            zeros = jnp.zeros((SMALL - GATE_ROWS, tokens), F32)
            turned_gates = jnp.transpose(jnp.concatenate([gate_all[r], zeros], 0))
            both = [
                jnp.sum(jnp.where(lanes == e * EXP_DEV + i, turned_gates, 0.0), -1, keepdims=True)
                for i in range(EXP_DEV)
            ]
            gates_ref[r] = jnp.where(lanes == 0, both[0], jnp.where(lanes == 1, both[1], 0.0))
        for copy in outs:
            copy.wait()
        wire.finish()

    def token_phase(w_gu, w_dn, cot_all, a_all, dgu_all, stage, ins, x_turned, cot_turned):
        expert.ins = ins
        scatter_dx.part = lambda r, half: x_all.at[r, :, pl.ds(half * width // 2, width // 2)]
        sources = [
            (w_gu_hbm.at[0], w_gu.at[0]),
            (w_dn_hbm.at[0], w_dn.at[0]),
            (d_out_hbm, cot_all.at[0]),
            (w_gu_hbm.at[1], w_gu.at[1]),
            (w_dn_hbm.at[1], w_dn.at[1]),
            (cot_hbm.at[1:], cot_all.at[1:]),
        ]
        loads = [
            pltpu.make_async_copy(source, dest, load_sems.at[n])
            for n, (source, dest) in enumerate(sources)
        ]
        for copy in loads[:5]:
            copy.start()
        step = 256
        wide = 512
        dg_lanes[...] = jnp.zeros_like(dg_lanes)

        def hidden_units(r, i, count=1):
            lane = lax.broadcasted_iota(jnp.int32, (1, SMALL), 1)
            here = pl.ds(r, count)
            flat = count * tokens

            @pl.loop(0, ff // step)
            def _(f):
                column = pl.multiple_of(f * step, step)
                rows = x_all[here].reshape(flat, width)
                grads = cot_all[here].reshape(flat, width)
                gate_part = dot_nn(rows, w_gu[i, :, pl.ds(column, step)])
                up_part = dot_nn(rows, w_gu[i, :, pl.ds(ff + column, step)])
                raw = dot_nt(grads, w_dn[i, pl.ds(column, step), :])
                gate = gates_ref[here].reshape(flat, SMALL)
                gate = jnp.sum(jnp.where(lane == i, gate, 0.0), -1, keepdims=True)
                sigma = jax.nn.sigmoid(gate_part)
                silu = gate_part * sigma
                act = silu * up_part
                lanes = lax.broadcasted_iota(jnp.int32, (flat, SMALL), 1)
                d_gate = jnp.where(
                    lanes == e * EXP_DEV + i, jnp.sum(act * raw, -1, keepdims=True), 0.0
                )
                dg_lanes[here] += d_gate.reshape(count, tokens, SMALL)

                def put(ref, first, values):
                    values = values.astype(BF16).reshape(count, tokens, step)
                    ref[here, :, pl.ds(pl.multiple_of(first, step), step)] = values

                put(a_all, i * ff + column, act * gate)
                d_act = raw * gate
                d_gate_part = d_act * up_part * sigma * (1.0 + gate_part * (1.0 - sigma))
                put(dgu_all, i * 2 * ff + column, d_gate_part)
                put(dgu_all, i * 2 * ff + ff + column, d_act * silu)

        def turn(rows, turned, r):
            @pl.loop(0, width // wide)
            def _(n):
                columns = pl.ds(pl.multiple_of(n * wide, wide), wide)
                turned[columns, pl.ds(r * tokens, tokens)] = jnp.transpose(rows[r, :, columns])

        def y_copy(r):
            return pltpu.make_async_copy(cot_all.at[r], y_hbm.at[r], out_sems.at[r])

        def outputs(r, count=1):
            here = pl.ds(r, count)
            flat = count * tokens

            @pl.loop(0, width // wide)
            def _(n):
                columns = pl.ds(pl.multiple_of(n * wide, wide), wide)
                low = dgu_all[here].reshape(flat, EXP_DEV * 2 * ff)
                d_rows = dot_nt(low[:, : 2 * ff], w_gu[0, columns, :])
                d_rows += dot_nt(low[:, 2 * ff :], w_gu[1, columns, :])
                weight = w_dn[:, :, columns].reshape(EXP_DEV * ff, wide)
                out = dot_nn(a_all[here].reshape(flat, EXP_DEV * ff), weight).astype(BF16)
                for k in range(count):
                    rows = slice(k * tokens, (k + 1) * tokens)
                    cot_all[r + k, :, columns] = out[rows]
                    if r == 0:
                        d_in_ref[:, columns] = d_rows
                    else:
                        x_all[r + k, :, columns] = d_rows[rows].astype(BF16)

            for k in range(r, r + count):
                y_copy(k).start()
                dg_part[k] = jnp.transpose(dg_lanes[k])[:GATE_ROWS]
                if k:
                    wire_1.start(dg_part.at[k], dg_land.at[k - 1], dg_slot + k - 1, ids[k])

        half_rows = width // nc // 2
        def where(k):
            high = lax.rem(lax.div(z, 2) + 1 + lax.div(k, 2), 2)
            return 2 * high + lax.rem(z + 1 + k, 2)

        def keep(i, k):
            slot = lax.rem(k, 2)
            return pltpu.make_async_copy(
                stage.at[slot, c], expert.part(base_hbm, where(k), i), stage_sems.at[slot]
            )

        def hand(i, k):
            return pltpu.make_async_remote_copy(
                src_ref=stage.at[lax.rem(k, 2), 1 - c],
                dst_ref=core_land.at[k],
                send_sem=hand_sends.at[i * nc + k],
                recv_sem=hand_recvs.at[i * nc + k],
                device_id=sibling,
                device_id_type=MESH,
            )

        def settle(i, k):
            hand(i, k).wait_recv()
            add_into(stage.at[lax.rem(k, 2), c], core_land.at[k])
            keep(i, k).start()

        def clear(i, k):
            keep(i, k).wait()
            hand(i, k).wait_send()

        def leave(i, r):
            if i == 0 and r == 2:
                expert.send(i, r, when=expert.end)
            elif i == 0 and r == 1 or r == 3:
                expert.send(i, r)
            elif r == 2:
                expert.send(i, r, when=bottom)
            elif r == 1:
                expert.send(i, r, when=even)

        def weight_grads(i, between=lambda k: None):
            @pl.loop(0, nc)
            def _(k):
                @pl.when(k >= 2)
                def _():
                    clear(i, k - 2)

                for n in (2, 3):

                    @pl.when(k == n)
                    def _(n=n):
                        leave(i, 5 - n)

                rows_at = pl.ds(pl.multiple_of(where(k) * 2 * half_rows, 2 * half_rows), 2 * half_rows)
                for first, rows, grad, start, count in (
                    (0, x_turned[rows_at, :], dgu_all, i * 2 * ff, 2),
                    (2 * ff, cot_turned[rows_at, :], a_all, i * ff, 1),
                ):

                    @pl.loop(0, count)
                    def _(n):
                        column = pl.multiple_of(n * ff, ff)
                        part = grad[:, :, pl.ds(pl.multiple_of(start + column, ff), ff)]
                        result = dot_nn(rows, part.reshape(blocks * tokens, ff)).astype(BF16)
                        stage[lax.rem(k, 2), :, :, pl.ds(pl.multiple_of(first + column, ff), ff)] = (
                            result.reshape(2, half_rows, ff)
                        )

                if i:

                    @pl.when(k == 0)
                    def _():
                        pl.semaphore_wait(credits.at[3], 1)

                hand(i, k).start()

                @pl.when(k >= 1)
                def _():
                    settle(i, k - 1)

                between(k)

        for copy in loads[:3]:
            copy.wait()
        gather_cot.complete()
        loads[5].start()
        for copy in loads[3:5]:
            copy.wait()

        @pl.loop(0, EXP_DEV)
        def _(i):
            hidden_units(0, i)

        gather.forward()
        turn(x_all, x_turned, 0)
        turn(cot_all, cot_turned, 0)
        outputs(0)
        loads[5].wait()
        for r in range(1, blocks):
            turn(cot_all, cot_turned, r)
        gather.near(1)
        gather.near(2)
        turn(x_all, x_turned, 1)
        turn(x_all, x_turned, 2)
        hidden_units(1, 0, 2)
        gather.far()
        turn(x_all, x_turned, 3)
        hidden_units(3, 0)
        weight_grads(0)
        hidden_units(1, 1, 2)
        clear(0, nc - 2)
        leave(0, 1)
        settle(0, nc - 1)
        pl.semaphore_signal(credits.at[3], inc=1, device_id=sibling, device_id_type=MESH)
        wire_x.finish()
        outputs(1, 2)
        scatter_dx.near(1)
        scatter_dx.near(2)
        hidden_units(3, 1)
        expert.relay_begin(0)
        outputs(3)
        scatter_dx.far()
        clear(0, nc - 1)
        expert.relay_add()

        def between(k):
            @pl.when(k == 0)
            def _():
                expert.relay_send(0)

            @pl.when(k == 1)
            def _():
                scatter_dx.relay()

        weight_grads(1, between)
        scatter_dx.total(d_in_ref)
        for r in (1, 2):
            pl.semaphore_signal(credits.at[r], inc=1, device_id=ids[r], device_id_type=MESH)
        settle(1, nc - 1)
        for k in (nc - 2, nc - 1):
            clear(1, k)
        leave(1, 1)
        for r in range(blocks):
            y_copy(r).wait()
        wire_1.finish()
        wire_c.finish()
        pl.semaphore_signal(credits.at[0], inc=1, device_id=sibling, device_id_type=MESH)

    def token_rows_phase(
        weight,
        grads_o,
        grads_q,
        x_ref,
        inputs_ref,
        query_ref,
        heads_ref,
        hidden_ref,
        d_hidden_ref,
        d_attn_ref,
        d_heads_ref,
        d_all_ref,
        rows_ref,
        dkv_acc,
        dkv_ref,
        y_relay,
        ins,
        out_wide,
    ):
        expert.ins, expert.out = ins, out_wide
        cot_ref, d_inputs_ref = d_heads_ref, hidden_ref
        scatter_y.part = lambda r, half: y_hbm.at[r, :, pl.ds(half * width // 2, width // 2)]
        y_loads = [
            pltpu.make_async_copy(scatter_y.part(2 - half, half), y_relay.at[half], y_sems.at[half])
            for half in range(2)
        ]
        for copy in y_loads:
            copy.start()
        planes = grads_o.shape[1]
        part = width // planes
        sources = (
            (hidden_hbm, hidden_ref),
            (d_out_hbm, cot_ref),
            (wo_hbm, weight),
            (heads_hbm, heads_ref),
            (query_hbm, query_ref),
            (x_hbm, x_ref),
            (inputs_hbm, inputs_ref),
        )
        loads = [
            pltpu.make_async_copy(source, dest, load_sems.at[4 + n])
            for n, (source, dest) in enumerate(sources)
        ]
        for copy in loads:
            copy.start()
        for r in (1, 2):
            scatter_y.near(r)
        scatter_y.far()

        def rows_scatter(buf, core, plane, lines, start, count, half):
            return RowsScatter(
                wire_2,
                buf,
                core,
                plane,
                lines,
                e,
                z,
                c,
                nc,
                start,
                count,
                half,
            )

        rows_of = part // 2
        scatter_o = rows_scatter(
            grads_o,
            x_all.at[:, pl.ds(0, rows_of)],
            lambda slot, half: dx_land.at[slot, pl.ds(0, rows_of)],
            lines_o,
            0,
            width,
            width // 2,
        )
        scatter_q = rows_scatter(
            grads_q,
            core_land.at[:, :, pl.ds(0, query_width)],
            lambda slot, half: plane_q.at[slot],
            lines_q,
            0,
            query_width,
            query_width // 2,
        )
        rest_half = rest // 256 * 128
        scatter_k = rows_scatter(
            grads_q,
            core_land.at[:, :, pl.ds(query_width, rest)],
            lambda slot, half: plane_k.at[
                slot, :, pl.ds(0, rest - rest_half if half else rest_half)
            ],
            lines_k,
            query_width,
            rest,
            rest_half,
        )
        scatter_kv = [
            LineSum(wire_2, lambda j, h=h: dkv_ref.at[h, j], dkv_land.at[h], z, nc, up=False)
            for h in range(KEY_VALUE_HEADS)
        ]

        for scatter in (scatter_o, scatter_q, scatter_k):
            scatter.line.clear()
        for line in scatter_kv:
            line.clear()

        loads[0].wait()
        loads[1].wait()
        hidden, d_in = hidden_ref[...], d_in_ref[...]
        scale2 = lax.rsqrt(jnp.mean(hidden * hidden, -1, keepdims=True) + EPSILON)
        scaled = d_in * gains_ref[1:2]
        mean = jnp.mean(scaled * hidden, -1, keepdims=True)
        d_hidden = cot_ref[...].astype(F32) + scale2 * scaled
        d_hidden = d_hidden - hidden * (scale2 * scale2 * scale2 * mean)
        d_hidden_ref[...] = d_hidden
        d_attn_ref[...] = d_hidden.astype(BF16)
        rows_ref[...] = jnp.zeros_like(rows_ref)
        rows_ref[experts + 1 : experts + 2, :] = jnp.sum(d_in * hidden * scale2, 0, keepdims=True)

        loads[2].wait()

        @pl.loop(0, query_width // 256)
        def _(n):
            columns = pl.ds(pl.multiple_of(n * 256, 256), 256)
            out = weight[:, :, :, :, columns].reshape(width, 256)
            d_heads_ref[:, columns] = dot_nn(d_attn_ref[...], out).astype(BF16)

        load_q = pltpu.make_async_copy(wq_hbm, weight, load_sems.at[0])
        load_q.start()
        loads[3].wait()

        def row_grads(buf, left, right, first, count, extra=None):
            @pl.loop(0, planes)
            def _(block):
                columns = pl.ds(pl.multiple_of(block * part, part), part)
                result = dot_tn(left[:, columns], right)
                if extra is not None:
                    result = result + extra(columns)
                result = result.astype(BF16).reshape(nc, 2, part // nc // 2, count)
                for half in range(2):
                    buf[half, block, :, pl.ds(first, count)] = result[:, half].reshape(
                        part // 2, count
                    )

        length = nc * tokens
        group = QUERY_HEADS // KEY_VALUE_HEADS
        loads[4].wait()
        dkv_acc[...] = jnp.zeros_like(dkv_acc)

        def attend(j, first, last):
            key = kv_ref[j, :, :, pl.ds(0, size)].reshape(length, size)
            value = kv_ref[j, :, :, pl.ds(size, size)].reshape(length, size)
            key_turned = jnp.transpose(key)

            @pl.loop(j * group + first, j * group + last)
            def _(h):
                columns = pl.ds(pl.multiple_of(h * size, size), size)
                query, grad = query_ref[:, columns], d_heads_ref[:, columns]
                scores = causal(dot_nt(key, query), z * tokens)
                largest = jnp.max(scores, 0, keepdims=True)
                expd = jnp.exp((scores - largest) * (size**-0.5))
                probs = expd * (1.0 / jnp.sum(expd, 0, keepdims=True))
                d_probs = dot_nt(value, grad)
                inner = jnp.sum(probs * d_probs, 0, keepdims=True)
                d_raw = (probs * (d_probs - inner) * (size**-0.5)).astype(BF16)
                d_query = jnp.transpose(dot_nn(key_turned, d_raw))
                d_query = d_query * cos_ref[...] - swap_halves(d_query) * sin_ref[...]
                d_all_ref[:, columns] = d_query.astype(BF16)
                dkv_acc[j, :, pl.ds(0, size)] += dot_nn(d_raw, query)
                dkv_acc[j, :, pl.ds(size, size)] += dot_nn(probs.astype(BF16), grad)

        def round_kv(j):
            for block in range(nc):
                rows = dkv_acc[j, pl.ds(block * tokens, tokens), :]
                dkv_ref[j, block] = rows.astype(BF16)

        def enter():
            pl.semaphore_wait(credits.at[1], 1)
            pl.semaphore_wait(credits.at[2], 1)

        attend(0, 0, group)
        round_kv(0)
        scatter_kv[0].send()
        attend(1, 0, group)
        round_kv(1)
        scatter_kv[1].send()
        expert.send(1, 2, when=top)
        expert.send(1, 1, when=odd)
        row_grads(grads_o, d_attn_ref, heads_ref[...], 0, width)
        pl.semaphore_wait(credits.at[0], 1)
        scatter_o.share()
        y_own = pltpu.make_async_copy(y_hbm.at[0], heads_ref, load_sems.at[2])
        y_own.start()
        for copy in y_loads:
            copy.wait()
        scatter_y.relay(lambda r, half: y_relay.at[half])
        scatter_o.merge(enter)

        for copy in loads[5:]:
            copy.wait()
        row_grads(grads_q, inputs_ref, d_all_ref[:, pl.ds(0, query_width)], 0, query_width)
        scatter_q.share()
        scatter_o.relay()
        expert.last(0, (sum_gu_hbm, sum_dn_hbm))
        expert.relay_begin(1)
        scatter_q.merge()
        expert.relay_add()
        for h in range(KEY_VALUE_HEADS):
            grad = scatter_kv[h].total()
            d_key = grad[:, :size]
            d_key = d_key * cos_ref[...] - swap_halves(d_key) * sin_ref[...]
            d_all_ref[:, pl.ds(query_width + h * size, size)] = d_key.astype(BF16)
            d_all_ref[:, pl.ds(query_width + key_width + h * size, size)] = grad[:, size:].astype(
                BF16
            )
        expert.relay_send(1)
        y_own.wait()
        hidden_ref[...] += heads_ref[...].astype(F32)
        scatter_y.total(hidden_ref)
        heads_ref[...] = hidden_ref[...].astype(BF16)
        layer_out = pltpu.make_async_copy(heads_ref, layer_hbm, out_sems.at[0])
        layer_out.start()

        total = dg_part[0]
        for r in (1, 2, 3):
            wire_1.arrived(dg_land.at[r - 1], dg_slot + r - 1, ids[r])
            total = total + dg_land[r - 1]
        gates = gate_all[0]
        d_logits = gates * (total - jnp.sum(gates * total, 0, keepdims=True))
        d_logits = jnp.concatenate(
            [d_logits, jnp.zeros((SMALL - d_logits.shape[0], tokens), F32)], 0
        )
        d_all_ref[:, pl.ds(qkv_width, SMALL)] = jnp.transpose(d_logits).astype(BF16)

        load_q.wait()

        @pl.loop(0, planes)
        def _(block):
            columns = pl.ds(pl.multiple_of(block * part, part), part)
            rows_q = weight[block].reshape(part, query_width)
            rows_k = wk_all[block].reshape(part, rest)
            d_inputs_ref[:, columns] = dot_nt(
                d_all_ref[:, pl.ds(0, query_width)], rows_q
            ) + dot_nt(d_all_ref[:, pl.ds(query_width, rest)], rows_k)

        rows = x_ref[...].astype(F32)
        scale1 = lax.rsqrt(jnp.mean(rows * rows, -1, keepdims=True) + EPSILON)
        d_inputs = d_inputs_ref[...]
        rows_ref[experts : experts + 1, :] = jnp.sum(d_inputs * rows * scale1, 0, keepdims=True)

        def extra(columns):
            small = jnp.transpose(rows_ref[:, columns])
            return jnp.concatenate([jnp.zeros((part, rest - SMALL), F32), small], 1)

        row_grads(
            grads_q, inputs_ref, d_all_ref[:, pl.ds(query_width, rest)], query_width, rest, extra
        )
        scatter_k.share()
        scatter_o.total()
        scatter_o.line.send()
        scatter_q.relay()
        scatter_k.merge()
        scaled = d_inputs_ref[...] * gains_ref[0:1]
        rows = x_ref[...].astype(F32)
        scale1 = lax.rsqrt(jnp.mean(rows * rows, -1, keepdims=True) + EPSILON)
        mean = jnp.mean(scaled * rows, -1, keepdims=True)
        d_x = d_hidden_ref[...] + scale1 * scaled - rows * (scale1 * scale1 * scale1 * mean)
        inputs_ref[...] = d_x.astype(BF16)
        d_x_out = pltpu.make_async_copy(inputs_ref, d_x_hbm, out_sems.at[1])
        d_x_out.start()
        scatter_q.total()
        scatter_q.line.send()
        scatter_k.relay()
        scatter_k.total()
        scatter_k.line.send()
        sum_o_ref[...] = scatter_o.line.total()
        expert.last(1, (sum_gu_hbm, sum_dn_hbm))
        sum_q_ref[:, pl.ds(0, query_width)] = scatter_q.line.total()
        sum_q_ref[:, pl.ds(query_width, rest)] = scatter_k.line.total()
        layer_out.wait()
        d_x_out.wait()
        wire_2.finish()
        expert.finish()

    held = EXP_DEV
    weight_shape = wq_hbm.shape
    pl.run_scoped(
        front_phase,
        pltpu.VMEM(weight_shape, BF16),
        pltpu.VMEM(weight_shape, BF16),
        pltpu.VMEM((tokens, width), BF16),
        pltpu.VMEM((tokens, width), BF16),
        pltpu.VMEM((tokens, query_width), BF16),
        pltpu.VMEM((tokens, query_width), BF16),
        pltpu.VMEM((tokens, width), F32),
        pltpu.VMEM((tokens, rest), F32),
        pltpu.VMEM((tokens, query_width), F32),
    )
    shard, step = width // nc // 2, 48
    pl.run_scoped(
        token_phase,
        pltpu.VMEM((held, width, 2 * ff), BF16),
        pltpu.VMEM((held, ff, width), BF16),
        pltpu.VMEM((blocks, tokens, width), BF16),
        pltpu.VMEM((blocks, tokens, held * ff), BF16),
        pltpu.VMEM((blocks, tokens, held * 2 * ff), BF16),
        pltpu.VMEM((2, 2, shard, grad_width // held), BF16),
        pltpu.VMEM((2, shard // step, step, grad_width // held), BF16),
        pltpu.VMEM((width, blocks * tokens), BF16),
        pltpu.VMEM((width, blocks * tokens), BF16),
    )
    rows_half = width // blocks // 2
    pl.run_scoped(
        token_rows_phase,
        pltpu.VMEM(weight_shape, BF16),
        pltpu.VMEM((2, blocks, rows_half, width), BF16),
        pltpu.VMEM((2, blocks, rows_half, qkv_width + SMALL), BF16),
        pltpu.VMEM((tokens, width), BF16),
        pltpu.VMEM((tokens, width), BF16),
        pltpu.VMEM((tokens, query_width), BF16),
        pltpu.VMEM((tokens, query_width), BF16),
        pltpu.VMEM((tokens, width), F32),
        pltpu.VMEM((tokens, width), F32),
        pltpu.VMEM((tokens, width), BF16),
        pltpu.VMEM((tokens, query_width), BF16),
        pltpu.VMEM((tokens, qkv_width + SMALL), BF16),
        pltpu.VMEM((SMALL, width), F32),
        pltpu.VMEM((KEY_VALUE_HEADS, nc * tokens, 2 * size), F32),
        pltpu.VMEM((KEY_VALUE_HEADS, nc, tokens, 2 * size), BF16),
        pltpu.VMEM((2, tokens, width // 2), BF16),
        pltpu.VMEM((4, shard // step, step, grad_width // held), BF16),
        pltpu.VMEM((2, step, grad_width // held), F32),
    )


def layer(operands, sizes):
    ne, nc, nd = sizes
    qkv_shard, x = operands[3], operands[6]
    w_dn = operands[9]
    tokens, width = x.shape
    held, ff = w_dn.shape[0], w_dn.shape[1]
    query_width = QUERY_HEADS * HEAD_DIMENSION
    rows, qkv_width = qkv_shard.shape
    rest = qkv_width - query_width + SMALL
    rest_half = rest // 256 * 128
    shard, grads = width // (nc * nd), held * 3 * ff
    kv_size = 2 * HEAD_DIMENSION
    weight = (ne, nc, nd, rows, query_width)
    shapes = [
        ((tokens, width), BF16),
        ((tokens, width), BF16),
        ((rows, qkv_width + SMALL), F32),
        ((rows, width), F32),
        ((held, shard, 2 * ff), F32),
        ((held, shard, ff), F32),
        ((nc, shard, grads), BF16),
        ((nc + 1, shard, grads), BF16),
        ((ne, tokens, width), BF16),
        (weight, BF16),
        (weight, BF16),
        ((ne, tokens, width), BF16),
        ((tokens, width), BF16),
        ((tokens, query_width), BF16),
        ((tokens, query_width), BF16),
        ((tokens, width), F32),
    ]
    vmem = pl.BlockSpec(memory_space=pltpu.VMEM)
    anywhere = pl.BlockSpec(memory_space=pl.ANY)
    units = nc * held
    sems = [120, 110, 6, 6, 6, 6, 10, 10, 64, 64, 2 * units, (nc + 1) * held, units, units, 2, 12, 6]
    return pl.pallas_call(
        functools.partial(layer_kernel, nc, EXP_DEV * ne),
        out_shape=[jax.ShapeDtypeStruct(*s) for s in shapes],
        in_specs=[vmem] * 6 + [anywhere] * (len(operands) - 6),
        out_specs=[anywhere] * 2 + [vmem] * 2 + [anywhere] * (len(shapes) - 4),
        scratch_shapes=[
            pltpu.VMEM((ne, nc, nd, rows, rest), BF16),
            pltpu.VMEM((KEY_VALUE_HEADS, nc, tokens, kv_size), BF16),
            pltpu.VMEM((ne, GATE_ROWS, tokens), F32),
            pltpu.VMEM((ne, tokens, SMALL), F32),
            pltpu.VMEM((8, width), F32),
            pltpu.VMEM((ne, tokens, width), BF16),
            pltpu.VMEM((6, tokens, width // 2), BF16),
            pltpu.VMEM((6, tokens, width // 2), BF16),
            pltpu.VMEM((nc, shard, grads // held), BF16),
            pltpu.VMEM((6, nc * rows, query_width // 2), BF16),
            pltpu.VMEM((6, nc * rows, rest - rest_half), BF16),
            pltpu.VMEM((nc, rows, width), BF16),
            pltpu.VMEM((nc, rows, query_width), BF16),
            pltpu.VMEM((nc, rows, rest), BF16),
            pltpu.VMEM((KEY_VALUE_HEADS, nc, tokens, kv_size), BF16),
            pltpu.VMEM((tokens, width), F32),
            pltpu.VMEM((ne, tokens, SMALL), F32),
            pltpu.VMEM((ne, GATE_ROWS, tokens), F32),
            pltpu.VMEM((ne - 1, GATE_ROWS, tokens), F32),
        ]
        + [pltpu.SemaphoreType.DMA((count,)) for count in sems]
        + [
            pltpu.SemaphoreType.DMA((20,)),
            pltpu.SemaphoreType.DMA((2,)),
            pltpu.SemaphoreType.REGULAR((4,)),
        ],
        compiler_params=pltpu.CompilerParams(
            collective_id=0, has_side_effects=True, vmem_limit_bytes=63 * MIB
        ),
    )(*operands)


def finish_kernel(experts, *refs):
    sources, dests = refs[:6], refs[6:12]
    router_ref, first_ref, second_ref = refs[12:]
    sum_q = sources[0]
    qkv_width = dests[0].shape[-1]
    dests[0][...] = sum_q[:, pl.ds(0, qkv_width)]
    for source, dest in zip(sources[1:], dests[1:]):
        dest[...] = source[...]
    small = sum_q[:, pl.ds(qkv_width, SMALL)]
    rows = small.shape[0]
    filled = jnp.concatenate([small, jnp.zeros((SMALL - rows, SMALL), F32)], 0)
    turned = jnp.transpose(filled)[:, :rows]
    router_ref[...] = turned[:experts]
    first_ref[...] = turned[experts : experts + 1]
    second_ref[...] = turned[experts + 1 : experts + 2]


def finish(sum_q, others, experts):
    rows, q_width = sum_q.shape
    vmem = pl.BlockSpec(memory_space=pltpu.VMEM)
    shapes = [jax.ShapeDtypeStruct((rows, q_width - SMALL), F32)]
    shapes += [jax.ShapeDtypeStruct(o.shape, o.dtype) for o in others]
    shapes += [jax.ShapeDtypeStruct((count, rows), F32) for count in (experts, 1, 1)]
    return pl.pallas_call(
        functools.partial(finish_kernel, experts),
        out_shape=shapes,
        in_specs=[vmem] * 6,
        out_specs=[vmem] * 9,
        compiler_params=pltpu.CompilerParams(vmem_limit_bytes=60 * MIB),
    )(sum_q, *others)


def local_plain(
    layer_input,
    gain_attn,
    query_key_value_weight,
    w_out,
    w_router,
    gain_ffn,
    w_gate_up,
    w_down,
    routes,
    d_out,
):
    tokens = layer_input.shape[1]
    model_width = layer_input.shape[2]
    ne, nc, nd = (lax.axis_size(a) for a in ("expert", "context", "dp"))
    expert_total = EXP_DEV * ne
    ff = w_down.shape[1]
    me = lax.axis_index("expert")
    first_row = lax.axis_index("context") * tokens
    query_width = QUERY_HEADS * HEAD_DIMENSION
    key_width = KEY_VALUE_HEADS * HEAD_DIMENSION
    qkv_width = query_width + 2 * key_width

    small = jnp.concatenate([w_router, gain_attn[:, None], gain_ffn[:, None]], -1)
    small = jnp.pad(small, ((0, 0), (0, 128 - small.shape[1])))
    gathered = gather_rows(jnp.concatenate([query_key_value_weight, small], -1))
    out_turned = gather_rows(w_out.T)
    qkv_weight = gathered[:, :qkv_width]
    router_weight = gathered[:, qkv_width : qkv_width + expert_total]
    gains = gathered[:, qkv_width + expert_total : qkv_width + expert_total + 2].T.astype(F32)
    gain_first, gain_second = gains[0], gains[1]
    cotangent_all = plane_gather(d_out[0])

    token_rows = layer_input[0].astype(F32)
    scale1 = lax.rsqrt(jnp.mean(token_rows * token_rows, -1, keepdims=True) + EPSILON)
    inputs1 = (token_rows * scale1 * gain_first).astype(BF16)
    query_key_value = dot_nn(inputs1, qkv_weight)
    cosine_values, sine_values = rope_tables(first_row + jnp.arange(tokens), HEAD_DIMENSION)
    rotated = rotate_half(
        query_key_value[:, : query_width + key_width].reshape(tokens, -1, HEAD_DIMENSION),
        cosine_values,
        sine_values,
    ).reshape(tokens, -1)
    query = rotated[:, :query_width].astype(BF16)
    key_value_local = jnp.concatenate(
        [rotated[:, query_width:], query_key_value[:, query_width + key_width :]], -1
    ).astype(BF16)
    key_value = line_gather(key_value_local, "context", both=False).reshape(nc * tokens, -1)
    first = first_row.astype(jnp.int32).reshape(1)
    heads = attend_forward(first, query, key_value)

    logits = dot_nn(inputs1, router_weight)
    chosen_ids = routes[0]
    picks = (chosen_ids[:, :, None] == jnp.arange(expert_total)[None, None, :]).astype(F32)
    chosen = jnp.sum(picks * logits[:, None, :], -1)
    gates = jax.nn.softmax(chosen, axis=-1)
    gate_dense = jnp.sum(picks * gates[:, :, None], 1).T
    gate_blocks = cube_gather(gate_dense, "expert", axis_masks("expert"))
    gate_local = jnp.concatenate(
        [lax.dynamic_slice_in_dim(b, me * EXP_DEV, EXP_DEV, 0) for b in gate_blocks], 1
    )

    attn = dot_nt(heads, out_turned)
    hidden = token_rows + attn
    scale2 = lax.rsqrt(jnp.mean(hidden * hidden, -1, keepdims=True) + EPSILON)
    expert_in = (hidden * scale2 * gain_second).astype(BF16)

    rows_all = plane_gather(expert_in)
    gate_up = jnp.einsum("td,edf->etf", rows_all, w_gate_up, preferred_element_type=F32)
    gate_part, up_part = gate_up[..., :ff], gate_up[..., ff:]
    sigma = jax.nn.sigmoid(gate_part)
    silu = gate_part * sigma
    act = silu * up_part
    gate_column = gate_local[:, :, None]
    act_gated = (act * gate_column).astype(BF16)
    partial_out = jnp.einsum("etf,efd->td", act_gated, w_down, preferred_element_type=F32)
    mixture = plane_scatter(partial_out.astype(BF16), tokens)
    layer_result = (hidden + mixture).astype(BF16)

    d_act_raw = jnp.einsum("td,efd->etf", cotangent_all, w_down, preferred_element_type=F32)
    d_gates_local = jnp.sum(d_act_raw * act, -1)
    d_act = d_act_raw * gate_column
    d_gate_part = d_act * up_part * sigma * (1.0 + gate_part * (1.0 - sigma))
    d_up_part = d_act * silu
    d_gate_up = jnp.concatenate([d_gate_part, d_up_part], -1).astype(BF16)
    d_rows = jnp.einsum("etf,edf->td", d_gate_up, w_gate_up, preferred_element_type=F32)
    grad_down = jnp.einsum("td,etf->edf", cotangent_all, act_gated, preferred_element_type=F32)
    grad_gate_up = jnp.einsum("td,etf->edf", rows_all, d_gate_up, preferred_element_type=F32)

    d_expert_in = plane_scatter(d_rows.astype(BF16), tokens)
    d_gate_blocks = d_gates_local.reshape(EXP_DEV, ne, tokens)
    d_gates_dense = jnp.zeros((expert_total, tokens), F32)
    for r in range(ne):
        arrived = d_gate_blocks[:, r]
        if r:
            arrived = exchange(arrived, "expert", r)
        d_gates_dense = lax.dynamic_update_slice(d_gates_dense, arrived, ((me ^ r) * EXP_DEV, 0))
    d_gates = jnp.sum(picks * d_gates_dense.T[:, None, :], -1)
    d_chosen = gates * (d_gates - jnp.sum(gates * d_gates, -1, keepdims=True))
    d_logits = jnp.sum(picks * d_chosen[:, :, None], 1).astype(BF16)
    grad_router = dot_tn(inputs1, d_logits)

    core = lax.axis_index("dp")
    part = model_width // (nc * nd)

    def scatter_experts(grad):
        blocks = grad.reshape(EXP_DEV, nc, nd, part, -1)
        mine = cube_scatter(
            [lax.dynamic_index_in_dim(blocks, core ^ r, 2, keepdims=False) for r in range(nd)],
            "dp",
            axis_masks("dp"),
        )
        return line_scatter(
            lambda j: lax.dynamic_index_in_dim(mine, j, 1, keepdims=False), "context"
        )

    sum_gate_up = scatter_experts(grad_gate_up)
    sum_down = jnp.swapaxes(scatter_experts(grad_down), 1, 2)

    cotangent = d_out[0].astype(F32)
    scaled2 = d_expert_in * gain_second
    d_hidden = (
        cotangent
        + scale2 * scaled2
        - hidden * (scale2 * scale2 * scale2) * jnp.mean(scaled2 * hidden, -1, keepdims=True)
    )
    grad_gain_second = jnp.sum(d_expert_in * hidden * scale2, 0)
    d_attn = d_hidden.astype(BF16)
    grad_out_turned = dot_tn(d_attn, heads)
    sum_out = scatter_rows(grad_out_turned).T
    d_heads = dot_nn(d_attn, out_turned).astype(BF16)
    d_query, d_key_all, d_value_all = attend_backward(first, query, key_value, d_heads)
    d_key_value_all = jnp.concatenate([d_key_all, d_value_all], -1).reshape(nc, tokens, -1)
    d_key_value = line_scatter(
        lambda j: lax.dynamic_index_in_dim(d_key_value_all, j, 0, keepdims=False),
        "context",
        up=False,
    )
    d_rotated = rotate_back(
        jnp.concatenate([d_query, d_key_value[:, :key_width]], -1).reshape(
            tokens, -1, HEAD_DIMENSION
        ),
        cosine_values,
        sine_values,
    ).reshape(tokens, -1)
    d_qkv = jnp.concatenate([d_rotated, d_key_value[:, key_width:]], -1).astype(BF16)
    d_inputs = dot_nt(d_qkv, qkv_weight) + dot_nt(d_logits, router_weight)
    grad_gain_first = jnp.sum(d_inputs * token_rows * scale1, 0)
    grad_qkv = dot_tn(inputs1, d_qkv)
    small_grads = jnp.concatenate(
        [grad_router, grad_gain_first[:, None], grad_gain_second[:, None]], -1
    )
    small_grads = jnp.pad(small_grads, ((0, 0), (0, 128 - small_grads.shape[1])))
    sum_rows = scatter_rows(jnp.concatenate([grad_qkv, small_grads], -1))
    sum_qkv = sum_rows[:, :qkv_width]
    sum_router = sum_rows[:, qkv_width : qkv_width + expert_total]
    sum_gain_first = sum_rows[:, qkv_width + expert_total]
    sum_gain_second = sum_rows[:, qkv_width + expert_total + 1]
    scaled1 = d_inputs * gain_first
    d_input_rows = (
        d_hidden
        + scale1 * scaled1
        - token_rows
        * (scale1 * scale1 * scale1)
        * jnp.mean(scaled1 * token_rows, -1, keepdims=True)
    ).astype(BF16)
    return (
        layer_result[None],
        d_input_rows[None],
        sum_gain_first,
        sum_qkv,
        sum_out,
        sum_router,
        sum_gain_second,
        sum_gate_up,
        sum_down,
    )


def local_fused(
    layer_input,
    gain_attn,
    query_key_value_weight,
    w_out,
    w_router,
    gain_ffn,
    w_gate_up,
    w_down,
    routes,
    d_out,
):
    tokens = layer_input.shape[1]
    ne, nc, nd = sizes = tuple(lax.axis_size(a) for a in ("expert", "context", "dp"))
    expert_total = EXP_DEV * ne
    first_row = lax.axis_index("context") * tokens
    query_width = QUERY_HEADS * HEAD_DIMENSION
    key_width = KEY_VALUE_HEADS * HEAD_DIMENSION
    qkv_width = query_width + 2 * key_width

    small = jnp.concatenate([w_router, gain_attn[:, None], gain_ffn[:, None]], -1)
    small = jnp.pad(small, ((0, 0), (0, SMALL - small.shape[1])))
    cosine_values, sine_values = rope_tables(first_row + jnp.arange(tokens), HEAD_DIMENSION)
    sine_values = sine_values * jnp.where(
        jnp.arange(HEAD_DIMENSION) < HEAD_DIMENSION // 2, -1.0, 1.0
    )
    layer_result, d_x, sum_rows, sum_out, sum_gate_up, sum_down = layer(
        (
            cosine_values,
            sine_values,
            routes[0].T,
            query_key_value_weight,
            small,
            w_out.T,
            layer_input[0],
            d_out[0],
            w_gate_up,
            w_down,
        ),
        sizes,
    )[:6]
    sum_qkv, layer_result, d_x, sum_gate_up, sum_down, sum_out, sum_router, *sum_gains = finish(
        sum_rows, (layer_result, d_x, sum_gate_up, sum_down, sum_out), expert_total
    )
    return (
        layer_result[None],
        d_x[None],
        sum_gains[0][0],
        sum_qkv,
        sum_out.T,
        sum_router.T,
        sum_gains[1][0],
        sum_gate_up,
        jnp.swapaxes(sum_down, 1, 2),
    )


def solution(mesh):
    in_specs = (
        P(("expert", "dp"), "context", None),
        P(("expert", "context", "dp")),
        P(("expert", "context", "dp"), None),
        P(None, ("expert", "context", "dp")),
        P(("expert", "context", "dp"), None),
        P(("expert", "context", "dp")),
        P("expert", None, None),
        P("expert", None, None),
        P(("expert", "dp"), "context", None),
        P(("expert", "dp"), "context", None),
    )
    out_specs = (
        P(("expert", "dp"), "context", None),
        P(("expert", "dp"), "context", None),
        P(("expert", "context", "dp")),
        P(("expert", "context", "dp"), None),
        P(None, ("expert", "context", "dp")),
        P(("expert", "context", "dp"), None),
        P(("expert", "context", "dp")),
        P("expert", ("context", "dp"), None),
        P("expert", None, ("context", "dp")),
    )
    sizes = tuple(mesh.shape[a] for a in ("expert", "context", "dp"))
    local = local_fused if sizes == (4, 4, 2) else local_plain
    return jax.shard_map(local, mesh=mesh, in_specs=in_specs, out_specs=out_specs, check_vma=False)
```

profile of v0, /device:TPU:0, one launch (start us, length us, event | category | flops | bytes accessed | tf_op | source)
XLA Modules:
  0.0 300.5 jit_solution(7637241601305638061)
XLA Ops:
  0.7 0.7 pad_maximum_fusion.1
  1.4 0.1 copy.22
  1.5 0.6 pad.4.small_ref
  2.1 0.5 multiply_sine_fusion
  2.7 0.8 pad_maximum_fusion
  3.5 291.8 %shard_map.169 = (bf16[256,1536]{1,0:T(8,128)(2,1)}, bf16[256,1536]{1,0:T(8,128)(2,1)}, f32[48,2176]{1,0:T(8,128)}, f32[48,1536]{1,0:T(8,128)}, f32[2,192,1536]{...) custom-call(f32[256,128]{1,0:T(8,128)} %get-tuple-element.41.cos_ref, ...), custom_call_target="tpu_custom_call" | custom-call | tf_op jit(solution)/shard_map/pallas_call | solution.py:1686
  295.3 5.2 %shard_map.170 = (f32[48,2048]{1,0:T(8,128)}, bf16[256,1536]{1,0:T(8,128)(2,1)}, bf16[256,1536]{1,0:T(8,128)(2,1)}, f32[2,192,1536]{2,1,0:T(8,128)}, f32[2,192,7...) custom-call(f32[48,2176]{1,0:T(8,128)} %get-tuple-element.24.refs_0_, ...), custom_call_target="tpu_custom_call" | custom-call | tf_op jit(solution)/shard_map/pallas_call | solution.py:1747
  (3 shorter events, 0.0 us)
where the time goes:
time: 301 us
  Pallas kernels  297 us (99%)
    pallas_call x1, Pallas kernels, layer(): pl.pallas_call(functools.partial(layer_kernel, nc, EXP_DEV * ne), out_sha...  292 us

commit v1 on v0

--- a/solution.py
+++ b/solution.py
@@ -654,7 +654,7 @@
         self.end = (z == 0) | (z == nc - 1)
         self.inner = jnp.logical_not(self.end)
         self.width = base.shape[-1] // EXP_DEV
-        self.first = wire.slots((nc + 1) * EXP_DEV)
+        self.first = wire.slots((nc + 2) * EXP_DEV)
         self.sent = []
 
     def part(self, ref, j, i):
@@ -699,9 +699,9 @@
 
     def copy(self, i, r, number):
         target, slot = flip(self.z, r), self.z
-        if r == 3:
+        if r > 1:
             target = jnp.where(self.end, flip(self.z, 1), target)
-            slot = jnp.where(self.end, self.nc, slot)
+            slot = jnp.where(self.end, self.nc + 3 - r, slot)
         return pltpu.make_async_remote_copy(
             src_ref=self.part(self.base, flip(self.z, r), i),
             dst_ref=self.part(self.land, slot, i),
@@ -724,63 +724,59 @@
         land = self.part(self.land, slot, i)
         self.wire.arrived(land, self.first + slot * EXP_DEV + i, {"context": self.z})
 
-    def relay_loads(self, i, p):
+    def relay_loads(self, i, r, p):
         step = self.ins.shape[2]
         rows = pl.ds(p * step, step)
-        sources = (self.part(self.base, flip(self.z, 2), i), self.part(self.land, self.nc, i))
+        far = self.nc + r - 2
+        sources = (self.part(self.base, flip(self.z, r), i), self.part(self.land, far, i))
         return [
-            pltpu.make_async_copy(
-                source.at[rows], self.ins.at[k, p], self.sems.at[4 * k + p]
-            )
+            pltpu.make_async_copy(source.at[rows], self.ins.at[k, p], self.sems.at[4 * k + p])
             for k, source in enumerate(sources)
         ]
 
-    def relay_store(self, i, p):
+    def relay_store(self, i, r, p):
         step = self.ins.shape[2]
-        mine = self.part(self.base, flip(self.z, 2), i).at[pl.ds(p * step, step)]
+        mine = self.part(self.base, flip(self.z, r), i).at[pl.ds(p * step, step)]
         return pltpu.make_async_copy(self.ins.at[0, p], mine, self.sems.at[16 + p])
 
     def relay_steps(self):
         return range(self.base.shape[1] // self.ins.shape[2])
 
-    def relay_begin(self, i):
-        self.relayed = i
-
+    def relay_begin(self, i, r):
         def begin():
-            self.arrived(self.nc, i)
+            self.arrived(self.nc + r - 2, i)
             for p in self.relay_steps():
-                for copy in self.relay_loads(i, p):
+                for copy in self.relay_loads(i, r, p):
                     copy.start()
 
         pl.when(self.inner)(begin)
 
-    def relay_add(self):
-        i = self.relayed
-
+    def relay_add(self, i, r):
         def add():
             for p in self.relay_steps():
-                for copy in self.relay_loads(i, p):
+                for copy in self.relay_loads(i, r, p):
                     copy.wait()
                 a, b = (self.ins[k, p].astype(F32) for k in range(2))
                 self.ins[0, p] = (a + b).astype(BF16)
-                self.relay_store(i, p).start()
+                self.relay_store(i, r, p).start()
 
         pl.when(self.inner)(add)
 
-    def relay_send(self, i):
+    def relay_send(self, i, r):
         def wait():
             for p in self.relay_steps():
-                self.relay_store(i, p).wait()
+                self.relay_store(i, r, p).wait()
 
         pl.when(self.inner)(wait)
-        self.send(i, 2, when=self.inner)
+        self.send(i, r, when=self.inner)
 
     def last(self, i, results):
         z = self.z
+        other = jnp.where(self.inner, flip(z, 3), flip(z, 2))
         sources = [self.part(self.base, z, i)]
-        for r in (1, 2):
-            self.arrived(flip(z, r), i)
-            sources.append(self.part(self.land, flip(z, r), i))
+        for source in (flip(z, 1), other):
+            self.arrived(source, i)
+            sources.append(self.part(self.land, source, i))
 
         def stores(rows, wide):
             pairs, first = [], 0
@@ -790,13 +786,7 @@
                 first += result.shape[-1]
             return pairs
 
-        pl.when(self.end)(lambda: self.combine(sources, stores))
-
-        def inner():
-            self.arrived(flip(z, 3), i)
-            self.combine(sources + [self.part(self.land, flip(z, 3), i)], stores)
-
-        pl.when(self.inner)(inner)
+        self.combine(sources, stores)
 
 
 def layer_kernel(
@@ -1195,14 +1185,12 @@
             hand(i, k).wait_send()
 
         def leave(i, r):
-            if i == 0 and r == 2:
+            if r == 1:
+                expert.send(i, r, when=even if i else None)
+            elif r == 3 or r == 2 and i == 0:
                 expert.send(i, r, when=expert.end)
-            elif i == 0 and r == 1 or r == 3:
-                expert.send(i, r)
             elif r == 2:
                 expert.send(i, r, when=bottom)
-            elif r == 1:
-                expert.send(i, r, when=even)
 
         def weight_grads(i, between=lambda k: None):
             @pl.loop(0, nc)
@@ -1283,22 +1271,31 @@
         scatter_dx.near(1)
         scatter_dx.near(2)
         hidden_units(3, 1)
-        expert.relay_begin(0)
+        expert.relay_begin(0, 2)
         outputs(3)
         scatter_dx.far()
         clear(0, nc - 1)
-        expert.relay_add()
+        expert.relay_add(0, 2)
 
         def between(k):
             @pl.when(k == 0)
             def _():
-                expert.relay_send(0)
+                expert.relay_send(0, 2)
 
             @pl.when(k == 1)
             def _():
                 scatter_dx.relay()
 
+            @pl.when(k == 2)
+            def _():
+                expert.relay_begin(0, 3)
+
+            @pl.when(k == 3)
+            def _():
+                expert.relay_add(0, 3)
+
         weight_grads(1, between)
+        expert.relay_send(0, 3)
         scatter_dx.total(d_in_ref)
         for r in (1, 2):
             pl.semaphore_signal(credits.at[r], inc=1, device_id=ids[r], device_id_type=MESH)
@@ -1501,7 +1498,9 @@
         scatter_kv[1].send()
         expert.send(1, 2, when=top)
         expert.send(1, 1, when=odd)
+        expert.relay_begin(1, 2)
         row_grads(grads_o, d_attn_ref, heads_ref[...], 0, width)
+        expert.relay_add(1, 2)
         pl.semaphore_wait(credits.at[0], 1)
         scatter_o.share()
         y_own = pltpu.make_async_copy(y_hbm.at[0], heads_ref, load_sems.at[2])
@@ -1509,6 +1508,7 @@
         for copy in y_loads:
             copy.wait()
         scatter_y.relay(lambda r, half: y_relay.at[half])
+        expert.relay_send(1, 2)
         scatter_o.merge(enter)
 
         for copy in loads[5:]:
@@ -1517,9 +1517,7 @@
         scatter_q.share()
         scatter_o.relay()
         expert.last(0, (sum_gu_hbm, sum_dn_hbm))
-        expert.relay_begin(1)
         scatter_q.merge()
-        expert.relay_add()
         for h in range(KEY_VALUE_HEADS):
             grad = scatter_kv[h].total()
             d_key = grad[:, :size]
@@ -1528,7 +1526,6 @@
             d_all_ref[:, pl.ds(query_width + key_width + h * size, size)] = grad[:, size:].astype(
                 BF16
             )
-        expert.relay_send(1)
         y_own.wait()
         hidden_ref[...] += heads_ref[...].astype(F32)
         scatter_y.total(hidden_ref)
@@ -1573,8 +1570,11 @@
         scatter_k.share()
         scatter_o.total()
         scatter_o.line.send()
+        expert.relay_begin(1, 3)
         scatter_q.relay()
+        expert.relay_add(1, 3)
         scatter_k.merge()
+        expert.relay_send(1, 3)
         scaled = d_inputs_ref[...] * gains_ref[0:1]
         rows = x_ref[...].astype(F32)
         scale1 = lax.rsqrt(jnp.mean(rows * rows, -1, keepdims=True) + EPSILON)
@@ -1669,7 +1669,7 @@
         ((held, shard, 2 * ff), F32),
         ((held, shard, ff), F32),
         ((nc, shard, grads), BF16),
-        ((nc + 1, shard, grads), BF16),
+        ((nc + 2, shard, grads), BF16),
         ((ne, tokens, width), BF16),
         (weight, BF16),
         (weight, BF16),
@@ -1682,7 +1682,7 @@
     vmem = pl.BlockSpec(memory_space=pltpu.VMEM)
     anywhere = pl.BlockSpec(memory_space=pl.ANY)
     units = nc * held
-    sems = [120, 110, 6, 6, 6, 6, 10, 10, 64, 64, 2 * units, (nc + 1) * held, units, units, 2, 12, 6]
+    sems = [120, 110, 6, 6, 6, 6, 10, 10, 64, 64, 2 * units, (nc + 2) * held, units, units, 2, 12, 6]
     return pl.pallas_call(
         functools.partial(layer_kernel, nc, EXP_DEV * ne),
         out_shape=[jax.ShapeDtypeStruct(*s) for s in shapes],

time: 301 us -> 294 us (0.977)
  Pallas kernels: 297 us -> 290 us
    pallas_call x1, Pallas kernels: 292 us -> 285 us  [layer(): pl.pallas_call(functools.partial(layer_kernel, nc, EXP_DEV * ne), out_sha...]
where the time goes in v1:
time: 294 us
  Pallas kernels  290 us (99%)
    pallas_call x1, Pallas kernels, layer(): pl.pallas_call(functools.partial(layer_kernel, nc, EXP_DEV * ne), out_sha...  285 us

profile of v1, /device:TPU:0, one launch (start us, length us, event | category | flops | bytes accessed | tf_op | source)
XLA Modules:
  0.0 293.6 jit_solution(9353346680856444221)
XLA Ops:
  0.7 0.7 pad_maximum_fusion.1
  1.4 0.1 copy.22
  1.5 0.6 pad.4.small_ref
  2.1 0.5 multiply_sine_fusion
  2.7 0.8 pad_maximum_fusion
  3.5 284.9 %shard_map.169 = (bf16[256,1536]{1,0:T(8,128)(2,1)}, bf16[256,1536]{1,0:T(8,128)(2,1)}, f32[48,2176]{1,0:T(8,128)}, f32[48,1536]{1,0:T(8,128)}, f32[2,192,1536]{...) custom-call(f32[256,128]{1,0:T(8,128)} %get-tuple-element.41.cos_ref, ...), custom_call_target="tpu_custom_call" | custom-call | tf_op jit(solution)/shard_map/pallas_call | solution.py:1686
  288.4 5.2 %shard_map.170 = (f32[48,2048]{1,0:T(8,128)}, bf16[256,1536]{1,0:T(8,128)(2,1)}, bf16[256,1536]{1,0:T(8,128)(2,1)}, f32[2,192,1536]{2,1,0:T(8,128)}, f32[2,192,7...) custom-call(f32[48,2176]{1,0:T(8,128)} %get-tuple-element.24.refs_0_, ...), custom_call_target="tpu_custom_call" | custom-call | tf_op jit(solution)/shard_map/pallas_call | solution.py:1747
  (3 shorter events, 0.0 us)
